TPU v7x, 32 devices: a whole 2x2x4 slice. The times are simulated.
32 devices in a mesh: win: 2 (over x), sta: 16 (over z, y, core).
Axes of the slice: x: 2, y: 2, z: 4, core: 2. Of those that a mesh axis runs over, the one named last changes fastest.
Arguments:
- records: bfloat16 [1024, 16384], P('win', 'sta'), parts along dimension 0, may hold values from -600 to 600
- filter_taps: bfloat16 [129], replicated, may hold values from -0.5 to 0.5
- ref_owner: int32 [4], P('win'), parts along dimension 0, may hold values from 0 to 15
- reference_station_order: int32 [4, 32], P('win'), parts along dimension 0, may hold values from 0 to 31, each once within a row
- pair_valid: int32 [4, 32, 512], P('win', None, 'sta'), parts along dimension 0, may hold values 0 or 1
Outputs:
- correlations: float32 [4, 32, 512, 256], P('win', None, 'sta'), parts along dimension 0
There are 2 independent parts, one for each index of `win`. A program takes and returns all parts, laid end to end along the dimension named above; an argument that names none is the same for every part. Nothing has to cross between parts.
Inputs may be any that keep to these rules, and one draw needn't show every extreme that they name: Each row of reference_station_order is a permutation of 0 .. 31.
All inputs are finite; a program needn't handle non-finite values. No bound on the sum of `pair_valid` on one device may be relied on, other than what follows from the above.
Results may differ from a plain program's by a relative error of at most 0.0073.
Values may be sent and summed in bfloat16 or wider, within the bound.
A program may use at most 128 MiB of HBM per device.

v0:
```python
import math

import jax
import jax.numpy as jnp
from jax import lax
from jax.sharding import PartitionSpec as P

NFFT = 1024
LAGS = 256
STEPS = 2


def from_root(block, axis, holder):
    block = jnp.where(lax.axis_index(axis) == holder, block, jnp.zeros_like(block))
    return lax.psum(block, axis)


def forward_matrix(length):
    time_index = jnp.arange(length, dtype=jnp.int32)[:, None]
    bin_index = jnp.arange(length // 2, dtype=jnp.int32)[None, :]
    angles = (time_index * bin_index % length).astype(jnp.float32) * (2.0 * math.pi / length)
    return jnp.concatenate([jnp.cos(angles), -jnp.sin(angles)], axis=1).astype(jnp.bfloat16)


def inverse_transform_matrix(length, lag_count, segments):
    bin_index = jnp.arange(length // 2, dtype=jnp.int32)[:, None]
    shifts = jnp.arange(lag_count, dtype=jnp.int32)[None, :] - lag_count // 2
    angles = (bin_index * shifts % length).astype(jnp.float32) * (2.0 * math.pi / length)
    factor = 1.0 / math.sqrt(segments * (length // 2))
    return jnp.concatenate([factor * jnp.cos(angles), -factor * jnp.sin(angles)], axis=0).astype(
        jnp.bfloat16
    )


def flatten_amplitudes(fourier_coefficients):
    bin_count = fourier_coefficients.shape[-1] // 2
    real_part = fourier_coefficients[..., :bin_count]
    imag_part = fourier_coefficients[..., bin_count:]
    energy = real_part * real_part + imag_part * imag_part
    water_level = jnp.mean(energy, axis=-1, keepdims=True)
    factor = lax.rsqrt(energy + water_level + 1e-06)
    return jnp.concatenate([real_part * factor, imag_part * factor], axis=-1).astype(jnp.bfloat16)


def spectra_of(station_rows, filter_taps):
    row_count, length = station_rows.shape
    tap_count = filter_taps.shape[0]
    margin = (tap_count - 1) // 2
    offsets = (
        jnp.arange(384, dtype=jnp.int32)[:, None]
        - jnp.arange(128, dtype=jnp.int32)[None, :]
        - 128
        + margin
    )
    match_flags = offsets[:, :, None] == jnp.arange(tap_count, dtype=jnp.int32)[None, None, :]
    banded = jnp.sum(
        jnp.where(match_flags, filter_taps.astype(jnp.float32)[None, None, :], 0.0), axis=2
    ).astype(jnp.bfloat16)
    padded = jnp.pad(station_rows, ((0, 0), (128, 128)))
    pieces = padded.reshape(row_count, length // 128 + 2, 128)
    windows = jnp.concatenate([pieces[:, :-2], pieces[:, 1:-1], pieces[:, 2:]], axis=2)
    filtered_signal = jnp.einsum(
        "nbu,uv->nbv", windows, banded, preferred_element_type=jnp.float32
    ).astype(jnp.bfloat16)
    segments = length // NFFT
    fourier_coefficients = jnp.dot(
        filtered_signal.reshape(row_count * segments, NFFT),
        forward_matrix(NFFT),
        preferred_element_type=jnp.float32,
    )
    return flatten_amplitudes(fourier_coefficients.reshape(row_count, segments, NFFT))


def correlate(chosen, resident, inverse):
    bin_count = chosen.shape[-1] // 2
    ref_stack = jnp.stack([chosen[..., :bin_count], chosen[..., bin_count:]], axis=2)
    direct = jnp.stack([resident[..., :bin_count], resident[..., bin_count:]], axis=2)
    rotated = jnp.stack([-resident[..., bin_count:], resident[..., :bin_count]], axis=2)
    real_sum = jnp.einsum("rgcf,sgcf->rsf", ref_stack, direct, preferred_element_type=jnp.float32)
    imag_sum = jnp.einsum("rgcf,sgcf->rsf", ref_stack, rotated, preferred_element_type=jnp.float32)
    cross = jnp.concatenate([real_sum, imag_sum], axis=-1).astype(jnp.bfloat16)
    ref_count = chosen.shape[0]
    own_count = resident.shape[0]
    lagged = jnp.dot(
        cross.reshape(ref_count * own_count, 2 * bin_count),
        inverse,
        preferred_element_type=jnp.float32,
    )
    return lagged.reshape(ref_count, own_count, inverse.shape[1])


def local(records, filter_taps, ref_owner, reference_station_order, pair_valid):
    station_rows = lax.all_to_all(records, "sta", split_axis=0, concat_axis=1, tiled=True)
    whitened = spectra_of(station_rows, filter_taps)
    inverse = inverse_transform_matrix(NFFT, LAGS, whitened.shape[1])
    results = []
    for running_total in range(STEPS):
        owner_index = ref_owner[running_total]
        ref_block = from_root(whitened, "sta", owner_index)
        chosen = jnp.take(ref_block, reference_station_order[running_total], axis=0)
        lagged = correlate(chosen, whitened, inverse)
        results.append(lagged * pair_valid[running_total].astype(jnp.float32)[:, :, None])
    return jnp.stack(results)


def solution(mesh):
    placed = (P("win", "sta"), P(), P("win"), P("win", None), P("win", None, "sta"))
    return jax.shard_map(
        local, mesh=mesh, in_specs=placed, out_specs=P("win", None, "sta", None), check_vma=False
    )
```

profile of v0, /device:TPU:0, one launch (start us, length us, event | category | flops | bytes accessed | tf_op | source)
XLA Modules:
  0.0 217.6 jit_solution(2442717941778114324)
XLA Ops:
  6.5 7.4 %all-to-all-start = ((bf16[16,32,1024]{2,1,0:T(8,128)(2,1)}), bf16[16,32,1024]{2,1,0:T(8,128)(2,1)S(1)}, u32[]{:S(2)}, u32[]{:S(2)}) async-start(bf16[16,32,1024]{2,1,0:T(8,128)(2,1)} %bitcast.83), calls=%async_computation | async-start | bytes 2097152 | tf_op jit(solution)/shard_map/all_to_all | solution.py:93
  14.6 1.3 fusion.56
  17.9 9.2 %negate_convert_fusion = (bf16[1024,512]{1,0:T(8,128)(2,1)S(1)}, bf16[1024,512]{1,0:T(8,128)(2,1)}) fusion(), kind=kLoop, calls=%fused_computation.37 | loop fusion | flops 8912896 | bytes 2097152 | tf_op jit(solution)/shard_map/convert.13
  27.1 2.6 %select_reduce_fusion = bf16[384,128]{1,0:T(8,128)(2,1)S(1)} fusion(f32[129]{0:T(256)S(1)} %convert_element_type.50, s32[384,128]{1,0:T(8,128)S(1)} %subtract_add_fusion), kind=kLoop, calls=%fused_computation.2 | loop fusion | flops 18972672 | bytes 295428 | tf_op jit(solution)/shard_map/reduce_sum | solution.py:56
  29.7 7.2 %all-to-all-done = bf16[16,32,1024]{2,1,0:T(8,128)(2,1)S(1)} async-done(((bf16[16,32,1024]{2,1,0:T(8,128)(2,1)}), bf16[16,32,1024]{2,1,0:T(8,128)(2,1)S(1)}, u32[]{:S(2)}, u32[]{:S(2)}) %all-to-all-start) | async-done | bytes 1048608 | tf_op jit(solution)/shard_map/all_to_all | solution.py:93
  40.6 2.8 %fusion.13 = f32[32,16,1024]{2,1,0:T(8,128)S(1)} fusion(bf16[32,16,1024]{2,1,0:T(8,128)(2,1)} %dot_general.27, bf16[1024,512]{1,0:T(8,128)(2,1)S(1)} %get-tuple-element.33, bf16[1024,512]{1,0:T(8,128)(2,1)} %get-tuple-element.34), kind=kOutput, calls=%fused_computation.25 | convolution fusion | flops 1077936128 | bytes 5242880 | tf_op jit(solution)/shard_map/dot_general | solution.py:66
  44.3 1.8 broadcast_select_fusion.3
  46.1 3.0 %multiply_convert_fusion.3 = (bf16[512,256]{1,0:T(8,128)(2,1)S(1)}, bf16[512,256]{1,0:T(8,128)(2,1)}) fusion(s32[256]{0:T(256)S(1)} %iota_add_fusion), kind=kLoop, calls=%fused_computation.72 | loop fusion | flops 2359296 | bytes 525312 | tf_op jit(solution)/shard_map/convert.4
  49.6 7.5 %copy.20 = bf16[32,16,2,512]{0,1,2,3:T(8,128)(2,1)} copy(bf16[32,16,2,512]{3,1,0,2:T(8,128)(2,1)S(1)} %get-tuple-element.23) | data formatting | bytes 2097152 | tf_op jit(solution)/shard_map/stack | solution.py:77
  57.0 7.4 %copy.22 = bf16[32,16,2,512]{0,1,2,3:T(8,128)(2,1)} copy(bf16[32,16,2,512]{3,1,0,2:T(8,128)(2,1)S(1)} %get-tuple-element.24) | data formatting | bytes 2097152 | tf_op jit(solution)/shard_map/stack | solution.py:78
  64.4 81.9 %all-reduce.4.cloned.1.call-done = (bf16[32,16,1024]{2,1,0:T(8,128)(2,1)}, bf16[32,16,1024]{2,1,0:T(8,128)(2,1)}) async-done(((bf16[32,16,1024]{2,1,0:T(8,128)(2,1)}, bf16[32,16,1024]{2,1,0:T(8,128)(2,1)}), (bf16[32,16,1024]{2,1,0:T(8,128)(2,1)}, bf16[32,16,1024]{2,1,0:T(8,128)(2,1)})) %all-reduce.4.cloned.1.call-update) | async-done | bytes 2097168 | tf_op jit(solution)/shard_map/psum | solution.py:15
  146.3 1.8 gather_fusion
  148.6 7.4 %copy.21 = bf16[32,16,2,512]{0,1,2,3:T(8,128)(2,1)} copy(bf16[32,16,2,512]{3,1,0,2:T(8,128)(2,1)S(1)} %pad_maximum_fusion.3) | data formatting | bytes 2097152 | tf_op jit(solution)/shard_map/stack | solution.py:76
  156.0 7.1 %fusion = bf16[32,32,512]{0,1,2:T(8,128)(2,1)} fusion(bf16[32,16,2,512]{0,1,2,3:T(8,128)(2,1)} %copy.20, bf16[32,16,2,512]{0,1,2,3:T(8,128)(2,1)} %copy.21), kind=kOutput, calls=%fused_computation.8 | convolution fusion | flops 34078720 | bytes 3145728 | tf_op jit(solution)/shard_map/rgcf,sgcf->rsf/dot_general | solution.py:79
  163.1 3.1 %fusion.1 = bf16[32,32,512]{0,1,2:T(8,128)(2,1)} fusion(bf16[32,16,2,512]{0,1,2,3:T(8,128)(2,1)S(1)} %copy-done, bf16[32,16,2,512]{0,1,2,3:T(8,128)(2,1)S(1)} %copy-done.3), kind=kOutput, calls=%fused_computation.9 | convolution fusion | flops 34078720 | bytes 3145728 | tf_op jit(solution)/shard_map/rgcf,sgcf->rsf/dot_general | solution.py:80
  167.2 7.5 %copy.27 = bf16[32,16,2,512]{0,1,2,3:T(8,128)(2,1)} copy(bf16[32,16,2,512]{3,1,0,2:T(8,128)(2,1)S(1)} %pad_maximum_fusion.5) | data formatting | bytes 2097152 | tf_op jit(solution)/shard_map/stack | solution.py:76
  174.6 7.1 %fusion.2 = bf16[32,32,512]{0,1,2:T(8,128)(2,1)} fusion(bf16[32,16,2,512]{0,1,2,3:T(8,128)(2,1)} %copy.20, bf16[32,16,2,512]{0,1,2,3:T(8,128)(2,1)} %copy.27), kind=kOutput, calls=%fused_computation.10 | convolution fusion | flops 34078720 | bytes 3145728 | tf_op jit(solution)/shard_map/rgcf,sgcf->rsf/dot_general | solution.py:79
  181.7 3.1 %fusion.3 = bf16[32,32,512]{0,1,2:T(8,128)(2,1)} fusion(bf16[32,16,2,512]{0,1,2,3:T(8,128)(2,1)S(1)} %copy-done.1, bf16[32,16,2,512]{0,1,2,3:T(8,128)(2,1)S(1)} %copy-done.2), kind=kOutput, calls=%fused_computation.11 | convolution fusion | flops 34078720 | bytes 3145728 | tf_op jit(solution)/shard_map/rgcf,sgcf->rsf/dot_general | solution.py:80
  184.8 5.2 %copy.24 = bf16[32,32,512]{2,1,0:T(8,128)(2,1)S(1)} copy(bf16[32,32,512]{0,1,2:T(8,128)(2,1)} %fusion) | data formatting | bytes 2097152 | tf_op jit(solution)/shard_map/rgcf,sgcf->rsf/transpose | solution.py:79
  190.1 6.0 %copy.25 = bf16[32,32,512]{2,1,0:T(8,128)(2,1)} copy(bf16[32,32,512]{0,1,2:T(8,128)(2,1)} %fusion.1) | data formatting | bytes 2097152 | tf_op jit(solution)/shard_map/rgcf,sgcf->rsf/transpose | solution.py:80
  196.1 5.2 %copy.30 = bf16[32,32,512]{2,1,0:T(8,128)(2,1)S(1)} copy(bf16[32,32,512]{0,1,2:T(8,128)(2,1)} %fusion.2) | data formatting | bytes 2097152 | tf_op jit(solution)/shard_map/rgcf,sgcf->rsf/transpose | solution.py:79
  201.3 5.2 %copy.31 = bf16[32,32,512]{2,1,0:T(8,128)(2,1)S(1)} copy(bf16[32,32,512]{0,1,2:T(8,128)(2,1)} %fusion.3) | data formatting | bytes 2097152 | tf_op jit(solution)/shard_map/rgcf,sgcf->rsf/transpose | solution.py:80
  206.6 2.0 fusion.39
  209.3 1.5 pad_maximum_fusion
  (42 shorter events, 8.6 us)
Async XLA Ops:
  6.5 30.3 %all-to-all-start = ((bf16[16,32,1024]{2,1,0:T(8,128)(2,1)}), bf16[16,32,1024]{2,1,0:T(8,128)(2,1)S(1)}, u32[]{:S(2)}, u32[]{:S(2)}) async-start(bf16[16,32,1024]{2,1,0:T(8,128)(2,1)} %bitcast.83), calls=%async_computation | async-start | bytes 2097152 | tf_op jit(solution)/shard_map/all_to_all | solution.py:93
  13.9 132.4 %all-reduce.4.cloned.1.call-start = ((), (), s32[]{:S(2)}) async-start(), calls=%async_computation.1 | async-start | bytes 4194304 | tf_op jit(solution)/shard_map/psum | solution.py:15
  44.0 2.1 copy-start.6
  156.0 7.1 %copy-start = (bf16[32,16,2,512]{0,1,2,3:T(8,128)(2,1)S(1)}, bf16[32,16,2,512]{0,1,2,3:T(8,128)(2,1)}, u32[]{:S(2)}) copy-start(bf16[32,16,2,512]{0,1,2,3:T(8,128)(2,1)} %copy.22) | copy-start | bytes 3145732
  156.0 7.1 %copy-start.3 = (bf16[32,16,2,512]{0,1,2,3:T(8,128)(2,1)S(1)}, bf16[32,16,2,512]{0,1,2,3:T(8,128)(2,1)}, u32[]{:S(2)}) copy-start(bf16[32,16,2,512]{0,1,2,3:T(8,128)(2,1)} %copy.21) | copy-start | bytes 3145732
  163.1 3.1 %copy-start.4 = (bf16[32,16,1024]{2,1,0:T(8,128)(2,1)S(1)}, bf16[32,16,1024]{2,1,0:T(8,128)(2,1)}, u32[]{:S(2)}) copy-start(bf16[32,16,1024]{2,1,0:T(8,128)(2,1)} %get-tuple-element.6) | copy-start | bytes 3145732
  174.6 7.1 %copy-start.1 = (bf16[32,16,2,512]{0,1,2,3:T(8,128)(2,1)S(1)}, bf16[32,16,2,512]{0,1,2,3:T(8,128)(2,1)}, u32[]{:S(2)}) copy-start(bf16[32,16,2,512]{0,1,2,3:T(8,128)(2,1)} %copy.22) | copy-start | bytes 3145732
  174.6 7.1 %copy-start.2 = (bf16[32,16,2,512]{0,1,2,3:T(8,128)(2,1)S(1)}, bf16[32,16,2,512]{0,1,2,3:T(8,128)(2,1)}, u32[]{:S(2)}) copy-start(bf16[32,16,2,512]{0,1,2,3:T(8,128)(2,1)} %copy.27) | copy-start | bytes 3145732
  206.6 2.0 copy-start.5
Sparse Core Ops, SparseCore 0:
  46.2 100.0 all-reduce.3
where the time goes:
time: 218 us
  waiting for transfers between devices  89 us (41%)
  local copies, waits for them, and re-layouts  58.2 us (27%)
  matrix products  26.8 us (12%)
  other arithmetic  21.3 us (10%)
  between operations  14.9 us (7%)
  starting transfers between devices  7.43 us (3%)
    psum x1, waiting for transfers between devices, from_root(): return lax.psum(block, axis)  81.9 us
    another operation x4, local copies, waits for them, and re-layouts, correlate(): jnp.stack([chosen[..., :bin_count], chosen[..., bin_count:]], axis=2)  15.1 us
    dot_general x2, matrix products, correlate(): jnp.einsum('rgcf,sgcf->rsf', ref_stack, direct, preferred_element_type=jn...  14.2 us
    another operation x2, other arithmetic  12.2 us
    transpose x2, local copies, waits for them, and re-layouts, correlate(): jnp.einsum('rgcf,sgcf->rsf', ref_stack, rotated, preferred_element_type=j...  11.3 us
    transpose x2, local copies, waits for them, and re-layouts, correlate(): jnp.einsum('rgcf,sgcf->rsf', ref_stack, direct, preferred_element_type=jn...  10.5 us
    another operation x1, local copies, waits for them, and re-layouts, correlate(): jnp.stack([resident[..., :bin_count], resident[..., bin_count:]], axis=2)  7.46 us
    another operation x1, local copies, waits for them, and re-layouts, correlate(): jnp.stack([-resident[..., bin_count:], resident[..., :bin_count]], axis=2)  7.42 us
  transfers between devices with their start and end apart: 2, of which 2 were waited for; matrix products, arithmetic and copies ran while one was open for 15% of the time, Pallas kernels for 0%

commit v1 on v0

--- a/solution.py
+++ b/solution.py
@@ -8,11 +8,6 @@
 NFFT = 1024
 LAGS = 256
 STEPS = 2
-
-
-def from_root(block, axis, holder):
-    block = jnp.where(lax.axis_index(axis) == holder, block, jnp.zeros_like(block))
-    return lax.psum(block, axis)
 
 
 def forward_matrix(length):
@@ -90,17 +85,17 @@
 
 
 def local(records, filter_taps, ref_owner, reference_station_order, pair_valid):
+    device_count = lax.axis_size("sta")
+    own_count = records.shape[0] // device_count
+    order = ref_owner[:, None] * own_count + reference_station_order
+    ref_rows = jnp.take(records, order.reshape(-1), axis=0)
+    ref_rows = lax.all_gather(ref_rows, "sta", axis=1, tiled=True)
     station_rows = lax.all_to_all(records, "sta", split_axis=0, concat_axis=1, tiled=True)
-    whitened = spectra_of(station_rows, filter_taps)
+    whitened = spectra_of(jnp.concatenate([station_rows, ref_rows], axis=0), filter_taps)
     inverse = inverse_transform_matrix(NFFT, LAGS, whitened.shape[1])
-    results = []
-    for running_total in range(STEPS):
-        owner_index = ref_owner[running_total]
-        ref_block = from_root(whitened, "sta", owner_index)
-        chosen = jnp.take(ref_block, reference_station_order[running_total], axis=0)
-        lagged = correlate(chosen, whitened, inverse)
-        results.append(lagged * pair_valid[running_total].astype(jnp.float32)[:, :, None])
-    return jnp.stack(results)
+    lagged = correlate(whitened[own_count:], whitened[:own_count], inverse)
+    lagged = lagged.reshape(STEPS, -1, own_count, LAGS)
+    return lagged * pair_valid.astype(jnp.float32)[..., None]
 
 
 def solution(mesh):

time: 218 us -> 153 us (0.70)
  waiting for transfers between devices: 89 us -> 31.2 us
  local copies, waits for them, and re-layouts: 58.2 us -> 49.3 us
  other arithmetic: 21.3 us -> 23.9 us
    psum x1 -> x0, waiting for transfers between devices: 81.9 us -> none  [from_root(): return lax.psum(block, axis)]
    all_gather x0 -> x1, waiting for transfers between devices: none -> 19 us  [local(): ref_rows = lax.all_gather(ref_rows, 'sta', axis=1, tiled=True)]
    dot_general x2 -> x1, matrix products: 14.2 us -> 6.97 us  [correlate(): jnp.einsum('rgcf,sgcf->rsf', ref_stack, direct, preferred_element_type=jn...]
    another operation x4 -> x3, local copies, waits for them, and re-layouts: 15.1 us -> 9.4 us  [correlate(): jnp.stack([chosen[..., :bin_count], chosen[..., bin_count:]], axis=2)]
    all_to_all x1, waiting for transfers between devices: 7.16 us -> 12.2 us  [local(): lax.all_to_all(records, 'sta', split_axis=0, concat_axis=1, tiled=True)]
    transpose x2 -> x1, local copies, waits for them, and re-layouts: 10.5 us -> 5.83 us  [correlate(): jnp.einsum('rgcf,sgcf->rsf', ref_stack, direct, preferred_element_type=jn...]
    transpose x2 -> x1, local copies, waits for them, and re-layouts: 11.3 us -> 6.96 us  [correlate(): jnp.einsum('rgcf,sgcf->rsf', ref_stack, rotated, preferred_element_type=j...]
    reshape x1, local copies, waits for them, and re-layouts: 0.56 us -> 4.27 us  [spectra_of(): pieces = padded.reshape(row_count, length // 128 + 2, 128)]
  transfers between devices with their start and end apart: 2 -> 2, of which waited for: 2 -> 2; matrix products, arithmetic and copies ran while one was open for 15% -> 10% of each run, Pallas kernels for 0% -> 0%
where the time goes in v1:
time: 153 us; the launch traced here: 152 us
  local copies, waits for them, and re-layouts  49.3 us (32%)
  waiting for transfers between devices  31.2 us (20%)
  matrix products  27 us (18%)
  other arithmetic  23.9 us (16%)
  between operations  13.5 us (9%)
  starting transfers between devices  7.4 us (5%)
    all_gather x1, waiting for transfers between devices, local(): ref_rows = lax.all_gather(ref_rows, 'sta', axis=1, tiled=True)  19 us
    another operation x3, other arithmetic  13.3 us
    all_to_all x1, waiting for transfers between devices, local(): lax.all_to_all(records, 'sta', split_axis=0, concat_axis=1, tiled=True)  12.2 us
    another operation x3, local copies, waits for them, and re-layouts, correlate(): jnp.stack([chosen[..., :bin_count], chosen[..., bin_count:]], axis=2)  9.4 us
    another operation x2, local copies, waits for them, and re-layouts, correlate(): jnp.stack([resident[..., :bin_count], resident[..., bin_count:]], axis=2)  7.65 us
    another operation x1, local copies, waits for them, and re-layouts, correlate(): jnp.stack([-resident[..., bin_count:], resident[..., :bin_count]], axis=2)  7.43 us
    all_to_all x1, starting transfers between devices, local(): lax.all_to_all(records, 'sta', split_axis=0, concat_axis=1, tiled=True)  7.4 us
    dot_general x1, matrix products, correlate(): jnp.einsum('rgcf,sgcf->rsf', ref_stack, rotated, preferred_element_type=j...  6.98 us
  transfers between devices with their start and end apart: 2, of which 2 were waited for; matrix products, arithmetic and copies ran while one was open for 10% of the time, Pallas kernels for 0%

profile of v1, /device:TPU:0, one launch (start us, length us, event | category | flops | bytes accessed | tf_op | source)
XLA Modules:
  0.0 152.3 jit_solution(6771176984339672772)
XLA Ops:
  8.2 2.2 %gather_fusion = bf16[64,1024]{1,0:T(8,128)(2,1)S(1)} fusion(bf16[512,1024]{1,0:T(8,128)(2,1)} %param.5, s32[1024]{0:T(1024)S(1)} %pad_clamp_fusion), kind=kCustom, calls=%fused_computation | custom fusion | bytes 262400 | tf_op jit(solution)/shard_map/jit(_take)/gather | solution.py:91
  11.1 7.4 %all-to-all-start = ((bf16[16,32,1024]{2,1,0:T(8,128)(2,1)}), bf16[16,32,1024]{2,1,0:T(8,128)(2,1)S(1)}, u32[]{:S(2)}, u32[]{:S(2)}) async-start(bf16[16,32,1024]{2,1,0:T(8,128)(2,1)} %bitcast.48), calls=%async_computation | async-start | bytes 2097152 | tf_op jit(solution)/shard_map/all_to_all | solution.py:93
  18.6 3.0 %multiply_convert_fusion.3 = (bf16[512,256]{1,0:T(8,128)(2,1)}, bf16[512,256]{1,0:T(8,128)(2,1)}) fusion(s32[256]{0:T(256)S(1)} %iota_add_fusion), kind=kLoop, calls=%fused_computation.60 | loop fusion | flops 2359296 | bytes 525312 | tf_op jit(solution)/shard_map/convert
  21.6 9.3 %negate_convert_fusion = (bf16[1024,512]{1,0:T(8,128)(2,1)}, bf16[1024,512]{1,0:T(8,128)(2,1)}) fusion(), kind=kLoop, calls=%fused_computation.39 | loop fusion | flops 8912896 | bytes 2097152 | tf_op jit(solution)/shard_map/convert.11
  30.9 2.6 %select_reduce_fusion = bf16[384,128]{1,0:T(8,128)(2,1)S(1)} fusion(f32[129]{0:T(256)S(1)} %convert_element_type.30, s32[384,128]{1,0:T(8,128)S(1)} %subtract_add_fusion), kind=kLoop, calls=%fused_computation.1 | loop fusion | flops 18972672 | bytes 295428 | tf_op jit(solution)/shard_map/reduce_sum | solution.py:51
  33.4 12.2 %all-to-all-done = bf16[16,32,1024]{2,1,0:T(8,128)(2,1)S(1)} async-done(((bf16[16,32,1024]{2,1,0:T(8,128)(2,1)}), bf16[16,32,1024]{2,1,0:T(8,128)(2,1)S(1)}, u32[]{:S(2)}, u32[]{:S(2)}) %all-to-all-start) | async-done | bytes 1048608 | tf_op jit(solution)/shard_map/all_to_all | solution.py:93
  45.7 19.0 %all-gather.2.cloned.1.call-done = bf16[64,16384]{1,0:T(8,128)(2,1)} async-done(((bf16[64,1024]{1,0:T(8,128)(2,1)}), bf16[64,16384]{1,0:T(8,128)(2,1)}) %all-gather.2.cloned.1.call-update) | async-done | bytes 2097168 | tf_op jit(solution)/shard_map/all_gather | solution.py:92
  64.7 3.3 %fusion.15 = bf16[96,16640]{1,0:T(8,128)(2,1)} fusion(bf16[64,16384]{1,0:T(8,128)(2,1)} %all-gather.2.cloned.1.call-done, bf16[32,16384]{1,0:T(8,128)(2,1)S(1)} %bitcast.50), kind=kLoop, calls=%fused_computation.22 | loop fusion | flops 14376960 | bytes 6340608 | tf_op jit(solution)/shard_map/concatenate | solution.py:94
  68.0 4.3 %reshape.87 = bf16[96,130,128]{2,1,0:T(8,128)(2,1)S(1)} reshape(bf16[96,16640]{1,0:T(8,128)(2,1)} %fusion.15) | data formatting | bytes 6389760 | tf_op jit(solution)/shard_map/reshape | solution.py:55
  72.3 2.0 %fusion.46 = (bf16[96,128,128]{2,1,0:T(8,128)(2,1)S(1)}, bf16[96,128,128]{2,1,0:T(8,128)(2,1)S(1)}, bf16[96,128,128]{2,1,0:T(8,128)(2,1)S(1)}) fusion(bf16[96,130,128]{2,1,0:T(8,128)(2,1)S(1)} %reshape.87), kind=kLoop, calls=%fused_computation.83 | loop fusion | bytes 18874368 | tf_op jit(solution)/shard_map/slice | solution.py:56
  74.3 3.0 %fusion.16 = bf16[96,128,128]{2,1,0:T(8,128)(2,1)S(1)} fusion(bf16[96,128,128]{2,1,0:T(8,128)(2,1)S(1)} %get-tuple-element.8, bf16[96,128,128]{2,1,0:T(8,128)(2,1)S(1)} %get-tuple-element.9, bf16[96,128,128]{2,1,0:T(8,128)(2,1)S(1)} %get-tuple-element.7, bf16[384,128]{1,0:T(8,128)(2,1)S(1)} %select_reduce_fusion), kind=kOutput, calls=%fused_computation.30 | convolution fusion | flops 1237843968 | bytes 12681216 | tf_op jit(solution)/shard_map/nbu,uv->nbv/dot_general | solution.py:57
  77.3 3.3 %dot_general.18 = bf16[96,16,1024]{2,1,0:T(8,128)(2,1)} reshape(bf16[96,128,128]{2,1,0:T(8,128)(2,1)S(1)} %fusion.16) | data formatting | bytes 6291456 | tf_op jit(solution)/shard_map/dot_general | solution.py:61
  80.6 5.9 %fusion.22 = f32[96,16,1024]{2,1,0:T(8,128)S(1)} fusion(bf16[96,16,1024]{2,1,0:T(8,128)(2,1)} %dot_general.18, bf16[1024,512]{1,0:T(8,128)(2,1)} %get-tuple-element.16, bf16[1024,512]{1,0:T(8,128)(2,1)} %get-tuple-element.17), kind=kOutput, calls=%fused_computation.35 | convolution fusion | flops 3225419776 | bytes 11534336 | tf_op jit(solution)/shard_map/dot_general | solution.py:61
  87.0 1.1 multiply_convert_fusion
  88.2 1.0 slice_bitcast_fusion
  90.5 7.6 %copy.28 = bf16[32,16,2,512]{0,1,2,3:T(8,128)(2,1)} copy(bf16[32,16,2,512]{3,1,0,2:T(8,128)(2,1)S(1)} %get-tuple-element.12) | data formatting | bytes 2097152 | tf_op jit(solution)/shard_map/stack | solution.py:72
  98.1 1.7 %pad_maximum_fusion = bf16[64,16,2,512]{3,1,0,2:T(8,128)(2,1)S(1)} fusion(bf16[64,16,1,512]{3,1,0,2:T(8,128)(2,1)} %slice_bitcast_fusion, bf16[64,16,1,512]{3,1,0,2:T(8,128)(2,1)} %slice_bitcast_fusion.1), kind=kLoop, calls=%fused_computation.38 | loop fusion | flops 1048576 | bytes 4194304 | tf_op jit(solution)/shard_map/stack | solution.py:71
  99.8 7.3 %copy.29 = bf16[64,16,2,512]{0,1,2,3:T(8,128)(2,1)} copy(bf16[64,16,2,512]{3,1,0,2:T(8,128)(2,1)S(1)} %pad_maximum_fusion) | data formatting | bytes 4194304 | tf_op jit(solution)/shard_map/stack | solution.py:71
  107.1 7.0 %fusion.9 = bf16[64,32,512]{0,1,2:T(8,128)(2,1)} fusion(bf16[32,16,2,512]{0,1,2,3:T(8,128)(2,1)} %copy.28, bf16[64,16,2,512]{0,1,2,3:T(8,128)(2,1)} %copy.29), kind=kOutput, calls=%fused_computation.16 | convolution fusion | flops 68157440 | bytes 5242880 | tf_op jit(solution)/shard_map/rgcf,sgcf->rsf/dot_general | solution.py:74
  114.1 5.8 %copy.30 = bf16[64,32,512]{2,1,0:T(8,128)(2,1)S(1)} copy(bf16[64,32,512]{0,1,2:T(8,128)(2,1)} %fusion.9) | data formatting | bytes 4194304 | tf_op jit(solution)/shard_map/rgcf,sgcf->rsf/transpose | solution.py:74
  119.9 7.4 %copy.31 = bf16[32,16,2,512]{0,1,2,3:T(8,128)(2,1)} copy(bf16[32,16,2,512]{3,1,0,2:T(8,128)(2,1)S(1)} %get-tuple-element.13) | data formatting | bytes 2097152 | tf_op jit(solution)/shard_map/stack | solution.py:73
  127.4 7.0 %fusion.10 = bf16[64,32,512]{0,1,2:T(8,128)(2,1)} fusion(bf16[32,16,2,512]{0,1,2,3:T(8,128)(2,1)} %copy.31, bf16[64,16,2,512]{0,1,2,3:T(8,128)(2,1)} %copy.29), kind=kOutput, calls=%fused_computation.17 | convolution fusion | flops 68157440 | bytes 5242880 | tf_op jit(solution)/shard_map/rgcf,sgcf->rsf/dot_general | solution.py:75
  134.4 7.0 %copy.33 = bf16[64,32,512]{2,1,0:T(8,128)(2,1)} copy(bf16[64,32,512]{0,1,2:T(8,128)(2,1)} %fusion.10) | data formatting | bytes 4194304 | tf_op jit(solution)/shard_map/rgcf,sgcf->rsf/transpose | solution.py:75
  141.3 4.2 %fusion.28 = f32[2,32,32,256]{3,2,1,0:T(8,128)} fusion(bf16[2,32,32,512]{3,2,1,0:T(8,128)(2,1)} %bitcast.52, bf16[2,32,32,512]{3,2,1,0:T(8,128)(2,1)S(1)} %bitcast.51, f32[2,32,32]{2,1,0:T(8,128)S(1)} %convert_element_type.35, bf16[512,256]{1,0:T(8,128)(2,1)S(1)} %copy-done.1, bf16[512,256]{1,0:T(8,128)(2,1)S(1)} %copy-done), kind=kOutput, calls=%fused_computation.44 | convolution fusion | flops 1083703296 | bytes 6823936 | tf_op jit(solution)/shard_map/dot_general | solution.py:79
  (29 shorter events, 4.3 us)
Async XLA Ops:
  6.5 11.9 %copy-start.3 = (bf16[129]{0:T(256)(128)(2,1)S(1)}, bf16[129]{0:T(256)(128)(2,1)}, u32[]{:S(2)}) copy-start(bf16[129]{0:T(256)(128)(2,1)} %param.6) | copy-start | bytes 778
  6.5 12.0 %copy-start.2 = (s32[2,32,32]{2,1,0:T(8,128)S(1)}, s32[2,32,32]{2,1,0:T(8,128)}, u32[]{:S(2)}) copy-start(s32[2,32,32]{2,1,0:T(8,128)} %param.9) | copy-start | bytes 24580
  6.5 58.2 %all-gather.2.cloned.1.call-start = ((), (), s32[]{:S(2)}) async-start(), calls=%async_computation.1 | async-start | bytes 2228224 | tf_op jit(solution)/shard_map/all_gather | solution.py:92
  11.1 34.6 %all-to-all-start = ((bf16[16,32,1024]{2,1,0:T(8,128)(2,1)}), bf16[16,32,1024]{2,1,0:T(8,128)(2,1)S(1)}, u32[]{:S(2)}, u32[]{:S(2)}) async-start(bf16[16,32,1024]{2,1,0:T(8,128)(2,1)} %bitcast.48), calls=%async_computation | async-start | bytes 2097152 | tf_op jit(solution)/shard_map/all_to_all | solution.py:93
  134.4 7.0 %copy-start = (bf16[512,256]{1,0:T(8,128)(2,1)S(1)}, bf16[512,256]{1,0:T(8,128)(2,1)}, u32[]{:S(2)}) copy-start(bf16[512,256]{1,0:T(8,128)(2,1)} %get-tuple-element.14) | copy-start | bytes 786436
  134.4 7.0 %copy-start.1 = (bf16[512,256]{1,0:T(8,128)(2,1)S(1)}, bf16[512,256]{1,0:T(8,128)(2,1)}, u32[]{:S(2)}) copy-start(bf16[512,256]{1,0:T(8,128)(2,1)} %get-tuple-element.15) | copy-start | bytes 786436
Sparse Core Ops, SparseCore 0:
  11.2 53.4 all-gather.1

commit v2 on v1

v2 whole, which is shorter than its diff:
```python
import math

import jax
import jax.numpy as jnp
import ml_dtypes
import numpy as np
from jax import lax
from jax.experimental import pallas as pl
from jax.experimental.pallas import tpu as pltpu
from jax.sharding import PartitionSpec as P

NFFT = 1024
LAGS = 256
BINS = NFFT // 2
LANES = 128
MIB = 1 << 20


def forward_padded():
    product = np.arange(BINS)[:, None] * np.arange(NFFT)[None, :] % NFFT
    angles = product * (2.0 * math.pi / NFFT)
    rows = np.concatenate([np.cos(angles), -np.sin(angles)], axis=0)
    return np.pad(rows, ((0, 0), (256, 256))).astype(np.float32).astype(ml_dtypes.bfloat16)


def inverse_rows(segments):
    product = np.arange(BINS)[None, :] * (np.arange(LAGS)[:, None] - LAGS // 2) % NFFT
    angles = product * (2.0 * math.pi / NFFT)
    factor = 1.0 / math.sqrt(segments * BINS)
    rows = np.concatenate([factor * np.cos(angles), -factor * np.sin(angles)], axis=1)
    return rows.astype(np.float32).astype(ml_dtypes.bfloat16)


def band(filter_taps):
    tap_count = filter_taps.shape[0]
    margin = (tap_count - 1) // 2
    offsets = (
        jnp.arange(LANES, dtype=jnp.int32)[None, :]
        - jnp.arange(3 * LANES, dtype=jnp.int32)[:, None]
        + LANES
        + margin
    )
    match = offsets[:, :, None] == jnp.arange(tap_count, dtype=jnp.int32)[None, None, :]
    return jnp.sum(
        jnp.where(match, filter_taps.astype(jnp.float32)[None, None, :], 0.0), axis=2
    ).astype(jnp.bfloat16)


def fold_kernel(forward_ref, band_ref, fold_ref):
    for j in range(fold_ref.shape[1] // LANES):
        fold_ref[:, j * LANES : (j + 1) * LANES] = jnp.dot(
            forward_ref[:, j * LANES : (j + 3) * LANES],
            band_ref[...],
            preferred_element_type=jnp.float32,
        ).astype(fold_ref.dtype)


def folded(filter_taps):
    return pl.pallas_call(
        fold_kernel,
        out_shape=jax.ShapeDtypeStruct((NFFT, NFFT + 2 * LANES), jnp.bfloat16),
        compiler_params=pltpu.CompilerParams(vmem_limit_bytes=32 * MIB),
    )(jnp.asarray(forward_padded()), band(filter_taps))


def main_kernel(fold_ref, own_ref, refs_ref, inv_ref, valid_ref, out_ref, x, y, w, o, v, z):
    segments, own, _ = own_ref.shape
    refs = refs_ref.shape[1]
    pairs = segments // 2
    depth = 2 * segments
    dot = lambda a, b, ca, cb: lax.dot_general(
        a, b, (((ca,), (cb,)), ((), ())), preferred_element_type=jnp.float32
    )

    for g in range(segments):
        base = (g % 2) * LANES
        places = ((0, own, own_ref), (own, own, own_ref), (2 * own, refs, refs_ref))
        for start, count, source in places:
            rows = slice(base + start, base + start + count)
            edge = jnp.zeros((count, LANES), x.dtype)
            x[g // 2, rows, LANES : LANES + NFFT] = source[g]
            x[g // 2, rows, :LANES] = source[g - 1, :, NFFT - LANES :] if g else edge
            x[g // 2, rows, LANES + NFFT :] = (
                source[g + 1, :, :LANES] if g + 1 < segments else edge
            )

    chunk = 64

    def transform(p, carry):
        y[...] = dot(fold_ref[...], x[p], 1, 1)
        lane = lax.broadcasted_iota(jnp.int32, (chunk, LANES), 1)
        turned = (lane >= own) & (lane < 2 * own)
        for h in range(2):
            columns = slice(h * LANES, (h + 1) * LANES)
            total = jnp.zeros((chunk, LANES), jnp.float32)
            for c in range(BINS // chunk):
                re = y[c * chunk : (c + 1) * chunk, columns]
                im = y[BINS + c * chunk : BINS + (c + 1) * chunk, columns]
                total += re * re + im * im
            water = jnp.sum(total, axis=0, keepdims=True) * (1.0 / BINS)
            for c in range(BINS // chunk):
                re = y[c * chunk : (c + 1) * chunk, columns]
                im = y[BINS + c * chunk : BINS + (c + 1) * chunk, columns]
                factor = lax.rsqrt(re * re + im * im + water + 1e-06)
                a, b = re * factor, im * factor
                at = c * chunk * depth + 2 * p + h
                w[pl.ds(at, chunk, stride=depth), :] = jnp.where(turned, -b, a)
                w[pl.ds(at + segments, chunk, stride=depth), :] = jnp.where(turned, a, b)
        return carry

    lax.fori_loop(0, pairs, transform, 0)

    group = LANES // depth
    both = 2 * own

    def cross(q, carry):
        t = w[pl.ds(pl.multiple_of(q * LANES, LANES), LANES), :]
        lane = lax.broadcasted_iota(jnp.int32, (LANES, LANES), 1)
        row = lax.broadcasted_iota(jnp.int32, (LANES, LANES), 0)
        left = t.T[:both].astype(jnp.bfloat16)
        twice = jnp.where(lane < refs, pltpu.roll(t, LANES - both, 1), t)
        right = jnp.concatenate(
            [
                jnp.where((row >= j * depth) & (row < (j + 1) * depth), twice, 0.0)
                for j in range(group)
            ],
            axis=1,
        ).astype(jnp.bfloat16)
        product = dot(left, right, 1, 0)
        for j in range(group):
            at = pl.multiple_of((q * group + j) * both, both)
            o[pl.ds(at, both), :] = product[:, j * LANES : (j + 1) * LANES]
        return carry

    lax.fori_loop(0, BINS // group, cross, 0, unroll=2)

    def lags(n, carry):
        lane = lax.broadcasted_iota(jnp.int32, (BINS, LANES), 1)
        for j in range(2):
            for c in range(2):
                at = c * own + 4 * n + 2 * j
                a = o[pl.ds(at, BINS, stride=both), :]
                b = o[pl.ds(at + 1, BINS, stride=both), :]
                v[c * BINS : (c + 1) * BINS, j * LANES : (j + 1) * LANES] = jnp.where(
                    lane < refs, a, b
                ).astype(v.dtype)
        lagged = dot(inv_ref[...], v[...], 1, 0) * valid_ref[n]
        turned = lagged.T
        for i in range(4):
            for h in range(LAGS // LANES):
                z[h, pl.ds(4 * n + i, refs, stride=own), :] = turned[
                    i * refs : (i + 1) * refs, h * LANES : (h + 1) * LANES
                ]
        return carry

    lax.fori_loop(0, own // 4, lags, 0)
    for h in range(LAGS // LANES):
        out_ref[:, h * LANES : (h + 1) * LANES] = z[h]


def compute(fold, own_rows, ref_rows, pair_valid):
    segments, own, _ = own_rows.shape
    refs = ref_rows.shape[1]
    valid = pair_valid.reshape(refs, own).astype(jnp.float32).T.reshape(own // 4, 1, 4 * refs)
    f32, bf16 = jnp.float32, jnp.bfloat16
    return pl.pallas_call(
        main_kernel,
        out_shape=jax.ShapeDtypeStruct((refs * own, LAGS), f32),
        scratch_shapes=[
            pltpu.VMEM((segments // 2, 2 * LANES, NFFT + 2 * LANES), bf16),
            pltpu.VMEM((NFFT, 2 * LANES), f32),
            pltpu.VMEM((BINS * 2 * segments, LANES), f32),
            pltpu.VMEM((BINS * 2 * own, LANES), f32),
            pltpu.VMEM((NFFT, 2 * LANES), bf16),
            pltpu.VMEM((LAGS // LANES, refs * own, LANES), f32),
        ],
        compiler_params=pltpu.CompilerParams(vmem_limit_bytes=52 * MIB),
    )(fold, own_rows, ref_rows, jnp.asarray(inverse_rows(segments)), valid)


def by_segment(blocks):
    devices, stations, samples = blocks.shape
    if samples == NFFT:
        return blocks
    return (
        blocks.transpose(1, 0, 2)
        .reshape(stations, devices * samples // NFFT, NFFT)
        .transpose(1, 0, 2)
    )


def local(records, filter_taps, ref_owner, reference_station_order, pair_valid):
    device_count = lax.axis_size("sta")
    stations, samples = records.shape
    own = stations // device_count
    order = ref_owner[:, None] * own + reference_station_order
    ref_rows = jnp.take(records, order.reshape(-1), axis=0)
    ref_rows = lax.all_gather(ref_rows, "sta", axis=0, tiled=False)
    own_rows = lax.all_to_all(
        records.reshape(device_count, own, samples), "sta", split_axis=0, concat_axis=0, tiled=True
    )
    out = compute(folded(filter_taps), by_segment(own_rows), by_segment(ref_rows), pair_valid)
    return out.reshape(pair_valid.shape + (LAGS,))


def solution(mesh):
    placed = (P("win", "sta"), P(), P("win"), P("win", None), P("win", None, "sta"))
    return jax.shard_map(
        local, mesh=mesh, in_specs=placed, out_specs=P("win", None, "sta", None), check_vma=False
    )
```

time: 153 us -> 121 us (0.79)
  Pallas kernels: 0 us -> 51.4 us
  local copies, waits for them, and re-layouts: 49.3 us -> 5.94 us
  matrix products: 27 us -> 0 us
  other arithmetic: 23.9 us -> 4.82 us
  waiting for transfers between devices: 31.2 us -> 37.7 us
    pallas_call x0 -> x2, Pallas kernels: none -> 51.4 us  [the longest x1 49.2 us: compute(): pl.pallas_call(main_kernel, out_shape=jax.ShapeDtypeStruct((refs * own, L...]
    dot_general x5 -> x0, matrix products: 27 us -> none  [the longest x1 6.98 us: correlate(): jnp.einsum('rgcf,sgcf->rsf', ref_stack, rotated, preferred_element_type=j...]
    another operation x6 -> x0, local copies, waits for them, and re-layouts: 24.5 us -> none  [the longest x3 9.4 us: correlate(): jnp.stack([chosen[..., :bin_count], chosen[..., bin_count:]], axis=2)]
    another operation x6 -> x0, other arithmetic: 15.3 us -> none
    transpose x2 -> x0, local copies, waits for them, and re-layouts: 12.8 us -> none  [the longest x1 6.96 us: correlate(): jnp.einsum('rgcf,sgcf->rsf', ref_stack, rotated, preferred_element_type=j...]
    all_to_all x1, waiting for transfers between devices: 12.2 us -> 18.6 us  [local(): lax.all_to_all(records.reshape(device_count, own, samples), 'sta', split_...]
    reshape x1, local copies, waits for them, and re-layouts: 4.27 us -> 0.08 us  [compute(): pair_valid.reshape(refs, own).astype(jnp.float32)]
    unnamed x8 -> x10, local copies, waits for them, and re-layouts: 0.01 us -> 3.47 us
  transfers between devices with their start and end apart: 2 -> 2, of which waited for: 2 -> 2; matrix products, arithmetic and copies ran while one was open for 10% -> 2% of each run, Pallas kernels for 0% -> 2%
where the time goes in v2:
time: 121 us
  Pallas kernels  51.4 us (42%)
  waiting for transfers between devices  37.7 us (31%)
  between operations  13.5 us (11%)
  starting transfers between devices  7.4 us (6%)
  local copies, waits for them, and re-layouts  5.94 us (5%)
  other arithmetic  4.82 us (4%)
    pallas_call x1, Pallas kernels, compute(): pl.pallas_call(main_kernel, out_shape=jax.ShapeDtypeStruct((refs * own, L...  49.2 us
    all_gather x1, waiting for transfers between devices, local(): ref_rows = lax.all_gather(ref_rows, 'sta', axis=0, tiled=False)  19 us
    all_to_all x1, waiting for transfers between devices, local(): lax.all_to_all(records.reshape(device_count, own, samples), 'sta', split_...  18.6 us
    all_to_all x1, starting transfers between devices, local(): lax.all_to_all(records.reshape(device_count, own, samples), 'sta', split_...  7.4 us
    unnamed x10, local copies, waits for them, and re-layouts  3.47 us
    reduce_sum x1, other arithmetic, band(): jnp.sum(jnp.where(match, filter_taps.astype(jnp.float32)[None, None, :],...  2.59 us
  transfers between devices with their start and end apart: 2, of which 2 were waited for; matrix products, arithmetic and copies ran while one was open for 2% of the time, Pallas kernels for 2%

profile of v2, /device:TPU:0, one launch (start us, length us, event | category | flops | bytes accessed | tf_op | source)
XLA Modules:
  0.0 120.8 jit_solution(14065282388231059199)
XLA Ops:
  6.5 0.0 copy-start.4
  6.5 0.0 copy-start.3
  6.5 0.0 all-gather.2.cloned.1.call-start
  6.5 0.7 broadcast_multiply_fusion
  7.2 0.7 broadcast_add_fusion
  8.0 0.1 reshape.91
  8.1 0.1 reshape.90
  8.2 2.2 %gather_fusion = bf16[64,1024]{1,0:T(8,128)(2,1)S(1)} fusion(bf16[512,1024]{1,0:T(8,128)(2,1)} %param.7, s32[1024]{0:T(1024)S(1)} %pad_clamp_fusion), kind=kCustom, calls=%fused_computation | custom fusion | bytes 262400 | tf_op jit(solution)/shard_map/jit(_take)/gather | solution.py:197
  10.3 0.7 bitcast_select_fusion
  11.1 0.0 all-gather.2.cloned.1.call-update
  11.1 7.4 %all-to-all-start = ((bf16[16,32,1024]{2,1,0:T(8,128)(2,1)}), bf16[16,32,1024]{2,1,0:T(8,128)(2,1)S(1)}, u32[]{:S(2)}, u32[]{:S(2)}) async-start(bf16[16,32,1024]{2,1,0:T(8,128)(2,1)} %bitcast.8), calls=%async_computation | async-start | bytes 2097152 | tf_op jit(solution)/shard_map/all_to_all | solution.py:199
  18.5 0.0 copy-done.4
  18.5 0.0 copy-done.3
  18.5 0.1 copy.10
  18.6 0.1 reshape.92.valid_ref
  18.7 2.6 %select_reduce_fusion.band_ref = bf16[384,128]{1,0:T(8,128)(2,1)S(1)} fusion(f32[129]{0:T(256)S(1)} %convert_element_type.12, s32[384,128]{1,0:T(8,128)S(1)} %subtract_add_fusion), kind=kLoop, calls=%fused_computation.1 | loop fusion | flops 18972672 | bytes 295428 | tf_op jit(solution)/shard_map/reduce_sum | solution.py:44
  21.3 1.9 %copy-done.1 = bf16[1024,1536]{1,0:T(8,128)(2,1)S(1)} copy-done((bf16[1024,1536]{1,0:T(8,128)(2,1)S(1)}, bf16[1024,1536]{1,0:T(8,128)(2,1)}, u32[]{:S(2)}) %copy-start.1) | copy-done | bytes 3145752
  23.3 2.2 %shard_map.73.fold_ref = bf16[1024,1280]{1,0:T(8,128)(2,1)S(1)} custom-call(bf16[1024,1536]{1,0:T(8,128)(2,1)S(1)} %copy-done.1, bf16[384,128]{1,0:T(8,128)(2,1)S(1)} %select_reduce_fusion.band_ref), custom_call_target="tpu_custom_call" | custom-call | tf_op jit(solution)/shard_map/pallas_call | solution.py:59
  25.5 0.0 copy-start
  25.5 1.5 %copy-done = bf16[1024,1280]{1,0:T(8,128)(2,1)} copy-done((bf16[1024,1280]{1,0:T(8,128)(2,1)}, bf16[1024,1280]{1,0:T(8,128)(2,1)S(1)}, u32[]{:S(2)}) %copy-start) | copy-done | bytes 2621464
  27.0 18.6 %all-to-all-done.own_ref = bf16[16,32,1024]{2,1,0:T(8,128)(2,1)S(1)} async-done(((bf16[16,32,1024]{2,1,0:T(8,128)(2,1)}), bf16[16,32,1024]{2,1,0:T(8,128)(2,1)S(1)}, u32[]{:S(2)}, u32[]{:S(2)}) %all-to-all-start) | async-done | bytes 1048608 | tf_op jit(solution)/shard_map/all_to_all | solution.py:199
  45.6 19.0 %all-gather.2.cloned.1.call-done.refs_ref = bf16[16,64,1024]{2,1,0:T(8,128)(2,1)} async-done(((bf16[1,64,1024]{2,1,0:T(8,128)(2,1)}), bf16[16,64,1024]{2,1,0:T(8,128)(2,1)}) %all-gather.2.cloned.1.call-update) | async-done | bytes 2097168 | tf_op jit(solution)/shard_map/all_gather | solution.py:198
  64.7 0.0 copy-done.2
  64.7 49.2 %shard_map.74 = f32[2048,256]{1,0:T(8,128)} custom-call(bf16[1024,1280]{1,0:T(8,128)(2,1)} %copy-done, bf16[16,32,1024]{2,1,0:T(8,128)(2,1)S(1)} %all-to-all-done.own_ref, bf16[16,64,1024]{2,1,0:T(8,128)(2,1)} %all-gather.2.cloned.1.call-done.refs_ref, bf16[256,1024]{1,0:T(8,128)(2,1)S(1)} %copy-done.2, f32[8,1,256]{2,1,0:T(1,128)S(1)} %reshape.92.valid_ref), custom_call_target="tpu_custom_call" | custom-call | tf_op jit(solution)/shard_map/pallas_call | solution.py:166
  (8 shorter events, 0.1 us)
Async XLA Ops:
  6.5 12.0 %copy-start.4 = (bf16[129]{0:T(256)(128)(2,1)S(1)}, bf16[129]{0:T(256)(128)(2,1)}, u32[]{:S(2)}) copy-start(bf16[129]{0:T(256)(128)(2,1)} %param.8) | copy-start | bytes 778
  6.5 12.0 %copy-start.3 = (s32[2,32,32]{2,1,0:T(8,128)S(1)}, s32[2,32,32]{2,1,0:T(8,128)}, u32[]{:S(2)}) copy-start(s32[2,32,32]{2,1,0:T(8,128)} %param.11) | copy-start | bytes 24580
  6.5 58.2 %all-gather.2.cloned.1.call-start = ((), (), s32[]{:S(2)}) async-start(), calls=%async_computation.1 | async-start | bytes 2228224 | tf_op jit(solution)/shard_map/all_gather | solution.py:198
  11.1 34.6 %all-to-all-start = ((bf16[16,32,1024]{2,1,0:T(8,128)(2,1)}), bf16[16,32,1024]{2,1,0:T(8,128)(2,1)S(1)}, u32[]{:S(2)}, u32[]{:S(2)}) async-start(bf16[16,32,1024]{2,1,0:T(8,128)(2,1)} %bitcast.8), calls=%async_computation | async-start | bytes 2097152 | tf_op jit(solution)/shard_map/all_to_all | solution.py:199
  21.3 1.9 %copy-start.1 = (bf16[1024,1536]{1,0:T(8,128)(2,1)S(1)}, bf16[1024,1536]{1,0:T(8,128)(2,1)}, u32[]{:S(2)}) copy-start(bf16[1024,1536]{1,0:T(8,128)(2,1)} %constant.28.clone.forward_ref) | copy-start | bytes 9437188
  23.3 41.4 %copy-start.2 = (bf16[256,1024]{1,0:T(8,128)(2,1)S(1)}, bf16[256,1024]{1,0:T(8,128)(2,1)}, u32[]{:S(2)}) copy-start(bf16[256,1024]{1,0:T(8,128)(2,1)} %constant.29.clone.inv_ref) | copy-start | bytes 1572868
  25.5 1.5 %copy-start = (bf16[1024,1280]{1,0:T(8,128)(2,1)}, bf16[1024,1280]{1,0:T(8,128)(2,1)S(1)}, u32[]{:S(2)}) copy-start(bf16[1024,1280]{1,0:T(8,128)(2,1)S(1)} %shard_map.73.fold_ref) | copy-start | bytes 7864324
Sparse Core Ops, SparseCore 0:
  11.2 53.4 all-gather.1

commit v3 on v2

--- a/solution.py
+++ b/solution.py
@@ -13,6 +13,7 @@
 LAGS = 256
 BINS = NFFT // 2
 LANES = 128
+SKEW = 8
 MIB = 1 << 20
 
 
@@ -103,9 +104,9 @@
                 im = y[BINS + c * chunk : BINS + (c + 1) * chunk, columns]
                 factor = lax.rsqrt(re * re + im * im + water + 1e-06)
                 a, b = re * factor, im * factor
-                at = c * chunk * depth + 2 * p + h
-                w[pl.ds(at, chunk, stride=depth), :] = jnp.where(turned, -b, a)
-                w[pl.ds(at + segments, chunk, stride=depth), :] = jnp.where(turned, a, b)
+                at = c * chunk * (depth + SKEW) + 2 * p + h
+                w[pl.ds(at, chunk, stride=depth + SKEW), :] = jnp.where(turned, -b, a)
+                w[pl.ds(at + segments, chunk, stride=depth + SKEW), :] = jnp.where(turned, a, b)
         return carry
 
     lax.fori_loop(0, pairs, transform, 0)
@@ -114,7 +115,11 @@
     both = 2 * own
 
     def cross(q, carry):
-        t = w[pl.ds(pl.multiple_of(q * LANES, LANES), LANES), :]
+        parts = [
+            w[pl.ds(pl.multiple_of((q * group + j) * (depth + SKEW), 8), depth), :]
+            for j in range(group)
+        ]
+        t = jnp.concatenate(parts, axis=0)
         lane = lax.broadcasted_iota(jnp.int32, (LANES, LANES), 1)
         row = lax.broadcasted_iota(jnp.int32, (LANES, LANES), 0)
         left = t.T[:both].astype(jnp.bfloat16)
@@ -128,19 +133,19 @@
         ).astype(jnp.bfloat16)
         product = dot(left, right, 1, 0)
         for j in range(group):
-            at = pl.multiple_of((q * group + j) * both, both)
+            at = pl.multiple_of((q * group + j) * (both + SKEW), 8)
             o[pl.ds(at, both), :] = product[:, j * LANES : (j + 1) * LANES]
         return carry
 
-    lax.fori_loop(0, BINS // group, cross, 0, unroll=2)
+    lax.fori_loop(0, BINS // group, cross, 0, unroll=8)
 
     def lags(n, carry):
         lane = lax.broadcasted_iota(jnp.int32, (BINS, LANES), 1)
         for j in range(2):
             for c in range(2):
                 at = c * own + 4 * n + 2 * j
-                a = o[pl.ds(at, BINS, stride=both), :]
-                b = o[pl.ds(at + 1, BINS, stride=both), :]
+                a = o[pl.ds(at, BINS, stride=both + SKEW), :]
+                b = o[pl.ds(at + 1, BINS, stride=both + SKEW), :]
                 v[c * BINS : (c + 1) * BINS, j * LANES : (j + 1) * LANES] = jnp.where(
                     lane < refs, a, b
                 ).astype(v.dtype)
@@ -153,7 +158,7 @@
                 ]
         return carry
 
-    lax.fori_loop(0, own // 4, lags, 0)
+    lax.fori_loop(0, own // 4, lags, 0, unroll=2)
     for h in range(LAGS // LANES):
         out_ref[:, h * LANES : (h + 1) * LANES] = z[h]
 
@@ -169,8 +174,8 @@
         scratch_shapes=[
             pltpu.VMEM((segments // 2, 2 * LANES, NFFT + 2 * LANES), bf16),
             pltpu.VMEM((NFFT, 2 * LANES), f32),
-            pltpu.VMEM((BINS * 2 * segments, LANES), f32),
-            pltpu.VMEM((BINS * 2 * own, LANES), f32),
+            pltpu.VMEM((BINS * (2 * segments + SKEW), LANES), f32),
+            pltpu.VMEM((BINS * (2 * own + SKEW), LANES), f32),
             pltpu.VMEM((NFFT, 2 * LANES), bf16),
             pltpu.VMEM((LAGS // LANES, refs * own, LANES), f32),
         ],

time: 121 us -> 98.6 us (0.81)
  Pallas kernels: 51.4 us -> 28.9 us
    pallas_call x1, Pallas kernels: 49.2 us -> 26.7 us  [compute(): pl.pallas_call(main_kernel, out_shape=jax.ShapeDtypeStruct((refs * own, L...]
  transfers between devices with their start and end apart: 2 -> 2, of which waited for: 2 -> 2; matrix products, arithmetic and copies ran while one was open for 2% -> 3% of each run, Pallas kernels for 2% -> 2%
where the time goes in v3:
time: 98.6 us; the launch traced here: 98.2 us
  waiting for transfers between devices  37.7 us (38%)
  Pallas kernels  28.9 us (29%)
  between operations  13.5 us (14%)
  starting transfers between devices  7.4 us (8%)
  local copies, waits for them, and re-layouts  5.94 us (6%)
  other arithmetic  4.82 us (5%)
    pallas_call x1, Pallas kernels, compute(): pl.pallas_call(main_kernel, out_shape=jax.ShapeDtypeStruct((refs * own, L...  26.7 us
    all_gather x1, waiting for transfers between devices, local(): ref_rows = lax.all_gather(ref_rows, 'sta', axis=0, tiled=False)  19 us
    all_to_all x1, waiting for transfers between devices, local(): lax.all_to_all(records.reshape(device_count, own, samples), 'sta', split_...  18.6 us
    all_to_all x1, starting transfers between devices, local(): lax.all_to_all(records.reshape(device_count, own, samples), 'sta', split_...  7.4 us
    unnamed x10, local copies, waits for them, and re-layouts  3.47 us
    reduce_sum x1, other arithmetic, band(): jnp.sum(jnp.where(match, filter_taps.astype(jnp.float32)[None, None, :],...  2.59 us
    pallas_call x1, Pallas kernels, folded(): pl.pallas_call(fold_kernel, out_shape=jax.ShapeDtypeStruct((NFFT, NFFT +...  2.21 us
    gather x1, local copies, waits for them, and re-layouts, local(): ref_rows = jnp.take(records, order.reshape(-1), axis=0)  2.16 us
  transfers between devices with their start and end apart: 2, of which 2 were waited for; matrix products, arithmetic and copies ran while one was open for 3% of the time, Pallas kernels for 2%

profile of v3, /device:TPU:0, one launch (start us, length us, event | category | flops | bytes accessed | tf_op | source)
XLA Modules:
  0.0 98.2 jit_solution(18149765767980897610)
XLA Ops:
  6.5 0.0 copy-start.4
  6.5 0.0 copy-start.3
  6.5 0.0 all-gather.2.cloned.1.call-start
  6.5 0.7 broadcast_multiply_fusion
  7.2 0.7 broadcast_add_fusion
  8.0 0.1 reshape.91
  8.1 0.1 reshape.90
  8.2 2.2 %gather_fusion = bf16[64,1024]{1,0:T(8,128)(2,1)S(1)} fusion(bf16[512,1024]{1,0:T(8,128)(2,1)} %param.7, s32[1024]{0:T(1024)S(1)} %pad_clamp_fusion), kind=kCustom, calls=%fused_computation | custom fusion | bytes 262400 | tf_op jit(solution)/shard_map/jit(_take)/gather | solution.py:202
  10.3 0.7 bitcast_select_fusion
  11.1 0.0 all-gather.2.cloned.1.call-update
  11.1 7.4 %all-to-all-start = ((bf16[16,32,1024]{2,1,0:T(8,128)(2,1)}), bf16[16,32,1024]{2,1,0:T(8,128)(2,1)S(1)}, u32[]{:S(2)}, u32[]{:S(2)}) async-start(bf16[16,32,1024]{2,1,0:T(8,128)(2,1)} %bitcast.8), calls=%async_computation | async-start | bytes 2097152 | tf_op jit(solution)/shard_map/all_to_all | solution.py:204
  18.5 0.0 copy-done.4
  18.5 0.0 copy-done.3
  18.5 0.1 copy.10
  18.6 0.1 reshape.92.valid_ref
  18.7 2.6 %select_reduce_fusion.band_ref = bf16[384,128]{1,0:T(8,128)(2,1)S(1)} fusion(f32[129]{0:T(256)S(1)} %convert_element_type.12, s32[384,128]{1,0:T(8,128)S(1)} %subtract_add_fusion), kind=kLoop, calls=%fused_computation.1 | loop fusion | flops 18972672 | bytes 295428 | tf_op jit(solution)/shard_map/reduce_sum | solution.py:45
  21.3 1.9 %copy-done.1 = bf16[1024,1536]{1,0:T(8,128)(2,1)S(1)} copy-done((bf16[1024,1536]{1,0:T(8,128)(2,1)S(1)}, bf16[1024,1536]{1,0:T(8,128)(2,1)}, u32[]{:S(2)}) %copy-start.1) | copy-done | bytes 3145752
  23.3 2.2 %shard_map.73.fold_ref = bf16[1024,1280]{1,0:T(8,128)(2,1)S(1)} custom-call(bf16[1024,1536]{1,0:T(8,128)(2,1)S(1)} %copy-done.1, bf16[384,128]{1,0:T(8,128)(2,1)S(1)} %select_reduce_fusion.band_ref), custom_call_target="tpu_custom_call" | custom-call | tf_op jit(solution)/shard_map/pallas_call | solution.py:60
  25.5 0.0 copy-start
  25.5 1.5 %copy-done = bf16[1024,1280]{1,0:T(8,128)(2,1)} copy-done((bf16[1024,1280]{1,0:T(8,128)(2,1)}, bf16[1024,1280]{1,0:T(8,128)(2,1)S(1)}, u32[]{:S(2)}) %copy-start) | copy-done | bytes 2621464
  27.0 18.6 %all-to-all-done.own_ref = bf16[16,32,1024]{2,1,0:T(8,128)(2,1)S(1)} async-done(((bf16[16,32,1024]{2,1,0:T(8,128)(2,1)}), bf16[16,32,1024]{2,1,0:T(8,128)(2,1)S(1)}, u32[]{:S(2)}, u32[]{:S(2)}) %all-to-all-start) | async-done | bytes 1048608 | tf_op jit(solution)/shard_map/all_to_all | solution.py:204
  45.6 19.0 %all-gather.2.cloned.1.call-done.refs_ref = bf16[16,64,1024]{2,1,0:T(8,128)(2,1)} async-done(((bf16[1,64,1024]{2,1,0:T(8,128)(2,1)}), bf16[16,64,1024]{2,1,0:T(8,128)(2,1)}) %all-gather.2.cloned.1.call-update) | async-done | bytes 2097168 | tf_op jit(solution)/shard_map/all_gather | solution.py:203
  64.7 0.0 copy-done.2
  64.7 26.7 %shard_map.74 = f32[2048,256]{1,0:T(8,128)} custom-call(bf16[1024,1280]{1,0:T(8,128)(2,1)} %copy-done, bf16[16,32,1024]{2,1,0:T(8,128)(2,1)S(1)} %all-to-all-done.own_ref, bf16[16,64,1024]{2,1,0:T(8,128)(2,1)} %all-gather.2.cloned.1.call-done.refs_ref, bf16[256,1024]{1,0:T(8,128)(2,1)S(1)} %copy-done.2, f32[8,1,256]{2,1,0:T(1,128)S(1)} %reshape.92.valid_ref), custom_call_target="tpu_custom_call" | custom-call | tf_op jit(solution)/shard_map/pallas_call | solution.py:171
  (8 shorter events, 0.1 us)
Async XLA Ops:
  6.5 12.0 %copy-start.4 = (bf16[129]{0:T(256)(128)(2,1)S(1)}, bf16[129]{0:T(256)(128)(2,1)}, u32[]{:S(2)}) copy-start(bf16[129]{0:T(256)(128)(2,1)} %param.8) | copy-start | bytes 778
  6.5 12.0 %copy-start.3 = (s32[2,32,32]{2,1,0:T(8,128)S(1)}, s32[2,32,32]{2,1,0:T(8,128)}, u32[]{:S(2)}) copy-start(s32[2,32,32]{2,1,0:T(8,128)} %param.11) | copy-start | bytes 24580
  6.5 58.2 %all-gather.2.cloned.1.call-start = ((), (), s32[]{:S(2)}) async-start(), calls=%async_computation.1 | async-start | bytes 2228224 | tf_op jit(solution)/shard_map/all_gather | solution.py:203
  11.1 34.6 %all-to-all-start = ((bf16[16,32,1024]{2,1,0:T(8,128)(2,1)}), bf16[16,32,1024]{2,1,0:T(8,128)(2,1)S(1)}, u32[]{:S(2)}, u32[]{:S(2)}) async-start(bf16[16,32,1024]{2,1,0:T(8,128)(2,1)} %bitcast.8), calls=%async_computation | async-start | bytes 2097152 | tf_op jit(solution)/shard_map/all_to_all | solution.py:204
  21.3 1.9 %copy-start.1 = (bf16[1024,1536]{1,0:T(8,128)(2,1)S(1)}, bf16[1024,1536]{1,0:T(8,128)(2,1)}, u32[]{:S(2)}) copy-start(bf16[1024,1536]{1,0:T(8,128)(2,1)} %constant.28.clone.forward_ref) | copy-start | bytes 9437188
  23.3 41.4 %copy-start.2 = (bf16[256,1024]{1,0:T(8,128)(2,1)S(1)}, bf16[256,1024]{1,0:T(8,128)(2,1)}, u32[]{:S(2)}) copy-start(bf16[256,1024]{1,0:T(8,128)(2,1)} %constant.29.clone.inv_ref) | copy-start | bytes 1572868
  25.5 1.5 %copy-start = (bf16[1024,1280]{1,0:T(8,128)(2,1)}, bf16[1024,1280]{1,0:T(8,128)(2,1)S(1)}, u32[]{:S(2)}) copy-start(bf16[1024,1280]{1,0:T(8,128)(2,1)S(1)} %shard_map.73.fold_ref) | copy-start | bytes 7864324
Sparse Core Ops, SparseCore 0:
  11.2 53.4 all-gather.1

commit v4 on v3

--- a/solution.py
+++ b/solution.py
@@ -200,9 +200,15 @@
     own = stations // device_count
     order = ref_owner[:, None] * own + reference_station_order
     ref_rows = jnp.take(records, order.reshape(-1), axis=0)
-    ref_rows = lax.all_gather(ref_rows, "sta", axis=0, tiled=False)
-    own_rows = lax.all_to_all(
-        records.reshape(device_count, own, samples), "sta", split_axis=0, concat_axis=0, tiled=True
+    halves = ref_rows.reshape(2, -1, samples)
+    spread = jnp.tile(halves, (device_count // 2, 1, 1))
+    blocks = jnp.concatenate([records.reshape(device_count, own, samples), spread], axis=1)
+    blocks = lax.all_to_all(blocks, "sta", split_axis=0, concat_axis=0, tiled=True)
+    own_rows, mine = blocks[:, :own], blocks[:, own:]
+    other = lax.ppermute(mine, "sta", [(i, i ^ 1) for i in range(device_count)])
+    first = lax.axis_index("sta") % 2 == 0
+    ref_rows = jnp.concatenate(
+        [jnp.where(first, mine, other), jnp.where(first, other, mine)], axis=1
     )
     out = compute(folded(filter_taps), by_segment(own_rows), by_segment(ref_rows), pair_valid)
     return out.reshape(pair_valid.shape + (LAGS,))

time: 98.6 us -> 98 us (level)
  blocking collectives: 0 us -> 54.8 us
  waiting for transfers between devices: 37.7 us -> 0.01 us
  between operations: 13.5 us -> 0.14 us
  starting transfers between devices: 7.4 us -> 0.77 us
  other arithmetic: 4.82 us -> 8.29 us
  local copies, waits for them, and re-layouts: 5.94 us -> 4.93 us
    all_to_all x0 -> x1, blocking collectives: none -> 54.8 us  [local(): lax.all_to_all(blocks, 'sta', split_axis=0, concat_axis=0, tiled=True)]
    all_gather x1 -> x0, waiting for transfers between devices: 19 us -> none  [local(): ref_rows = lax.all_gather(ref_rows, 'sta', axis=0, tiled=False)]
    all_to_all x1 -> x0, waiting for transfers between devices: 18.6 us -> none  [local(): lax.all_to_all(records.reshape(device_count, own, samples), 'sta', split_...]
    all_to_all x1 -> x0, starting transfers between devices: 7.4 us -> none  [local(): lax.all_to_all(records.reshape(device_count, own, samples), 'sta', split_...]
    select_n x0 -> x1, other arithmetic: none -> 2.23 us  [local(): jnp.where(first, mine, other)]
    unnamed x10 -> x16, local copies, waits for them, and re-layouts: 3.47 us -> 1.36 us
    concatenate x0 -> x2, other arithmetic: none -> 1.85 us  [the longest x1 1.57 us: local(): jnp.concatenate([jnp.where(first, mine, other), jnp.where(first, other, m...]
    slice x0 -> x1, local copies, waits for them, and re-layouts: none -> 1.07 us  [local(): own_rows, mine = (blocks[:, :own], blocks[:, own:])]
  transfers between devices with their start and end apart: 2 -> 1, of which waited for: 2 -> 0; matrix products, arithmetic and copies ran while one was open for 3% -> 3% of each run, Pallas kernels for 2% -> 2%
where the time goes in v4:
time: 98 us; the launch traced here: 97.8 us
  blocking collectives  54.8 us (56%)
  Pallas kernels  28.9 us (29%)
  other arithmetic  8.29 us (8%)
  local copies, waits for them, and re-layouts  4.93 us (5%)
    all_to_all x1, blocking collectives, local(): lax.all_to_all(blocks, 'sta', split_axis=0, concat_axis=0, tiled=True)  54.8 us
    pallas_call x1, Pallas kernels, compute(): pl.pallas_call(main_kernel, out_shape=jax.ShapeDtypeStruct((refs * own, L...  26.7 us
    reduce_sum x1, other arithmetic, band(): jnp.sum(jnp.where(match, filter_taps.astype(jnp.float32)[None, None, :],...  2.59 us
    select_n x1, other arithmetic, local(): jnp.where(first, mine, other)  2.23 us
    pallas_call x1, Pallas kernels, folded(): pl.pallas_call(fold_kernel, out_shape=jax.ShapeDtypeStruct((NFFT, NFFT +...  2.22 us
    gather x1, local copies, waits for them, and re-layouts, local(): ref_rows = jnp.take(records, order.reshape(-1), axis=0)  2.15 us
  transfers between devices with their start and end apart: 1, of which 0 were waited for; matrix products, arithmetic and copies ran while one was open for 3% of the time, Pallas kernels for 2%

profile of v4, /device:TPU:0, one launch (start us, length us, event | category | flops | bytes accessed | tf_op | source)
XLA Modules:
  0.0 97.8 jit_solution(12989960909306436260)
XLA Ops:
  0.0 0.7 broadcast_multiply_fusion
  0.7 0.8 compare_and_fusion
  1.5 0.1 reshape.79
  1.6 2.2 %gather_fusion = bf16[64,1024]{1,0:T(8,128)(2,1)S(1)} fusion(bf16[512,1024]{1,0:T(8,128)(2,1)} %param.7, s32[1024]{0:T(1024)S(1)} %pad_clamp_fusion), kind=kCustom, calls=%fused_computation | custom fusion | bytes 262400 | tf_op jit(solution)/shard_map/jit(_take)/gather | solution.py:202
  3.8 0.1 broadcast_select_fusion.2
  3.8 0.1 tile.8
  4.0 0.3 pad_maximum_fusion
  4.3 0.0 copy-start.7
  4.3 0.0 copy-start.6
  4.3 0.0 copy-start.1
  4.3 54.8 %all_to_all.5 = bf16[16,64,1024]{2,1,0:T(8,128)(2,1)S(1)} all-to-all(bf16[16,64,1024]{2,1,0:T(8,128)(2,1)S(1)} %pad_maximum_fusion), channel_id=1, replica_groups=mesh['win'=2,'sta'=16] {'sta'}, dimensions={0} | all-to-all | bytes 4194304 | tf_op jit(solution)/shard_map/all_to_all | solution.py:206
  59.1 1.3 %copy-done.3 = bf16[16,64,1024]{2,1,0:T(8,128)(2,1)} copy-done((bf16[16,64,1024]{2,1,0:T(8,128)(2,1)}, bf16[16,64,1024]{2,1,0:T(8,128)(2,1)S(1)}, u32[]{:S(2)}) %copy-start.3) | copy-done | bytes 2097176
  60.4 1.1 %slice.11 = bf16[16,32,1024]{2,1,0:T(8,128)(2,1)} slice(bf16[16,64,1024]{2,1,0:T(8,128)(2,1)S(1)} %all_to_all.5), slice={[0:16], [32:64], [0:1024]} | slice | bytes 2097152 | tf_op jit(solution)/shard_map/slice | solution.py:207
  61.5 0.8 collective-permute-start
  62.3 0.1 copy.9
  62.3 0.1 reshape.80.valid_ref
  62.4 0.0 copy-start.4
  62.4 2.6 %select_reduce_fusion.band_ref = bf16[384,128]{1,0:T(8,128)(2,1)S(1)} fusion(f32[129]{0:T(256)S(1)} %convert_element_type.12, s32[384,128]{1,0:T(8,128)S(1)} %subtract_add_fusion), kind=kLoop, calls=%fused_computation.1 | loop fusion | flops 18972672 | bytes 295428 | tf_op jit(solution)/shard_map/reduce_sum | solution.py:45
  65.0 2.2 %shard_map.73.fold_ref = bf16[1024,1280]{1,0:T(8,128)(2,1)S(1)} custom-call(bf16[1024,1536]{1,0:T(8,128)(2,1)S(1)} %copy-done.1, bf16[384,128]{1,0:T(8,128)(2,1)S(1)} %select_reduce_fusion.band_ref), custom_call_target="tpu_custom_call" | custom-call | tf_op jit(solution)/shard_map/pallas_call | solution.py:60
  67.3 0.0 collective-permute-done
  67.3 2.2 %broadcast_select_fusion.1 = (bf16[16,32,1024]{2,1,0:T(8,128)(2,1)S(1)}, bf16[16,32,1024]{2,1,0:T(8,128)(2,1)S(1)}, bf16[16,32,1024]{2,1,0:T(8,128)(2,1)S(1)}) fusion(bf16[16,32,1024]{2,1,0:T(8,128)(2,1)} %collective-permute-done, pred[]{:T(512)S(6)} %eq.21, bf16[16,64,1024]{2,1,0:T(8,128)(2,1)S(1)} %copy-done.4), kind=kLoop, calls=%fused_computation.6 | loop fusion | flops 1048576 | bytes 6291457 | tf_op jit(solution)/shard_map/jit(_where)/select_n | solution.py:211
  69.5 0.0 copy-start.2
  69.5 1.6 %pad_maximum_fusion.1.refs_ref = bf16[16,64,1024]{2,1,0:T(8,128)(2,1)} fusion(bf16[16,32,1024]{2,1,0:T(8,128)(2,1)S(1)} %get-tuple-element.8, bf16[16,32,1024]{2,1,0:T(8,128)(2,1)S(1)} %get-tuple-element.7), kind=kLoop, calls=%fused_computation.4 | loop fusion | flops 4194304 | bytes 4194304 | tf_op jit(solution)/shard_map/concatenate | solution.py:210
  71.1 26.7 %shard_map.74 = f32[2048,256]{1,0:T(8,128)} custom-call(bf16[1024,1280]{1,0:T(8,128)(2,1)} %copy-done, bf16[16,32,1024]{2,1,0:T(8,128)(2,1)S(1)} %get-tuple-element.9.own_ref, bf16[16,64,1024]{2,1,0:T(8,128)(2,1)} %pad_maximum_fusion.1.refs_ref, bf16[256,1024]{1,0:T(8,128)(2,1)S(1)} %copy-done.2, f32[8,1,256]{2,1,0:T(1,128)S(1)} %reshape.80.valid_ref), custom_call_target="tpu_custom_call" | custom-call | tf_op jit(solution)/shard_map/pallas_call | solution.py:171
  (15 shorter events, 0.1 us)
Async XLA Ops:
  0.0 4.0 %copy-start.5 = (bf16[512,1024]{1,0:T(8,128)(2,1)S(1)}, bf16[512,1024]{1,0:T(8,128)(2,1)}, u32[]{:S(2)}) copy-start(bf16[512,1024]{1,0:T(8,128)(2,1)} %param.7) | copy-start | bytes 3145732
  4.3 58.0 %copy-start.7 = (bf16[129]{0:T(256)(128)(2,1)S(1)}, bf16[129]{0:T(256)(128)(2,1)}, u32[]{:S(2)}) copy-start(bf16[129]{0:T(256)(128)(2,1)} %param.8) | copy-start | bytes 778
  4.3 58.0 %copy-start.6 = (s32[2,32,32]{2,1,0:T(8,128)S(1)}, s32[2,32,32]{2,1,0:T(8,128)}, u32[]{:S(2)}) copy-start(s32[2,32,32]{2,1,0:T(8,128)} %param.11) | copy-start | bytes 24580
  4.3 60.7 %copy-start.1 = (bf16[1024,1536]{1,0:T(8,128)(2,1)S(1)}, bf16[1024,1536]{1,0:T(8,128)(2,1)}, u32[]{:S(2)}) copy-start(bf16[1024,1536]{1,0:T(8,128)(2,1)} %constant.45.clone.forward_ref) | copy-start | bytes 9437188
  59.1 1.3 %copy-start.3 = (bf16[16,64,1024]{2,1,0:T(8,128)(2,1)}, bf16[16,64,1024]{2,1,0:T(8,128)(2,1)S(1)}, u32[]{:S(2)}) copy-start(bf16[16,64,1024]{2,1,0:T(8,128)(2,1)S(1)} %all_to_all.5) | copy-start | bytes 6291460
  61.5 5.8 %collective-permute-start = (bf16[16,32,1024]{2,1,0:T(8,128)(2,1)}, bf16[16,32,1024]{2,1,0:T(8,128)(2,1)}, u32[]{:S(2)}, u32[]{:S(2)}) collective-permute-start(bf16[16,32,1024]{2,1,0:T(8,128)(2,1)} %slice.11), channel_id=1, source_target_pairs={{0,1},{1,0},{2,3},{3,2},{4,5},{5,4},{6,7},{7,6},{8,9},{9,8},{10,11... | collective-permute-start | bytes 3145736 | tf_op jit(solution)/shard_map/ppermute | solution.py:208
  62.4 4.9 %copy-start.4 = (bf16[16,64,1024]{2,1,0:T(8,128)(2,1)S(1)}, bf16[16,64,1024]{2,1,0:T(8,128)(2,1)}, u32[]{:S(2)}) copy-start(bf16[16,64,1024]{2,1,0:T(8,128)(2,1)} %copy-done.3) | copy-start | bytes 6291460
  67.3 2.3 %copy-start = (bf16[1024,1280]{1,0:T(8,128)(2,1)}, bf16[1024,1280]{1,0:T(8,128)(2,1)S(1)}, u32[]{:S(2)}) copy-start(bf16[1024,1280]{1,0:T(8,128)(2,1)S(1)} %shard_map.73.fold_ref) | copy-start | bytes 7864324
  69.5 1.6 %copy-start.2 = (bf16[256,1024]{1,0:T(8,128)(2,1)S(1)}, bf16[256,1024]{1,0:T(8,128)(2,1)}, u32[]{:S(2)}) copy-start(bf16[256,1024]{1,0:T(8,128)(2,1)} %constant.46.clone.inv_ref) | copy-start | bytes 1572868
